TPU v7x, 32 devices: a whole 2x2x4 slice. The times are simulated.
32 devices in a mesh: ctx: 4 (over y, core), uly: 8 (over z, x).
Axes of the slice: x: 2, y: 2, z: 4, core: 2. Of those that a mesh axis runs over, the one named last changes fastest.
Arguments:
- query: bfloat16 [4096, 5120], P(('ctx', 'uly')), may hold values from -8 to 8
- key: bfloat16 [4096, 5120], P(('ctx', 'uly')), may hold values from -8 to 8
- value: bfloat16 [4096, 5120], P(('ctx', 'uly')), may hold values from -6 to 6
- dout: bfloat16 [4096, 5120], P(('ctx', 'uly')), may hold values from -6 to 6
- tile_mask: int32 [40, 32, 5], replicated, may hold values from 0 to 1, as said below
Outputs:
- grad_query: bfloat16 [4096, 5120], P(('ctx', 'uly'))
- grad_key: bfloat16 [4096, 5120], P(('ctx', 'uly'))
- grad_value: bfloat16 [4096, 5120], P(('ctx', 'uly'))
Inputs may be any that keep to these rules, and one draw needn't show every extreme that they name: `tile_mask`: the tile of a block with itself (offset 2) is active for every head and block.
All inputs are finite; a program needn't handle non-finite values.
Results may differ from a plain program's by a relative error of at most 0.0053.
Values may be sent and summed in bfloat16 or wider, within the bound.
A program may use at most 128 MiB of HBM per device.

v0:
```python
import math

import jax
import jax.numpy as jnp
from jax import lax
from jax.sharding import PartitionSpec as P

BLK = 128


def padded_2(x, sides, width):
    for axis, dim in sides:
        size, length = (lax.axis_size(axis), x.shape[dim])
        up = [(i, (i + 1) % size) for i in range(size - 1)]
        down = [(j, i) for i, j in up]
        last = lax.slice_in_dim(x, length - width, length, axis=dim)
        initial = lax.slice_in_dim(x, 0, width, axis=dim)
        before = lax.ppermute(last, axis, up)
        after = lax.ppermute(initial, axis, down)
        x = jnp.concatenate([before, x, after], axis=dim)
    return x


def passed_along(value, axis, steps):
    count = lax.axis_size(axis)
    initial, last = (max(0, -steps), min(count, count - steps))
    return lax.ppermute(value, axis, [(source, source + steps) for source in range(initial, last)])


def window_stack(blocks, block_count, tile_span):
    return jnp.stack([blocks[offset : offset + block_count] for offset in range(tile_span)], 1)


def attend_grad(query_matrix, key_ext, value_ext, output_gradient, active, logit_scale):
    block_count = query_matrix.shape[0]
    tile_span = active.shape[1]
    windowed_keys = window_stack(key_ext, block_count, tile_span)
    windowed_values = window_stack(value_ext, block_count, tile_span)
    attention_logits = (
        jnp.einsum(
            "mip,mejp->meij", query_matrix, windowed_keys, preferred_element_type=jnp.float32
        )
        * logit_scale
    )
    masked = jnp.where(active[:, :, None, None], attention_logits, -jnp.inf)
    row_top = jnp.max(masked, axis=(1, 3), keepdims=True)
    weights = jnp.exp(masked - row_top)
    denom_sum = jnp.sum(weights, axis=(1, 3), keepdims=True)
    prob_f = weights / denom_sum
    backward_probability = prob_f.astype(jnp.bfloat16)
    probability_gradient = jnp.einsum(
        "mip,mejp->meij", output_gradient, windowed_values, preferred_element_type=jnp.float32
    )
    row_delta = jnp.sum(prob_f * probability_gradient, axis=(1, 3), keepdims=True)
    score_gradient = (prob_f * (probability_gradient - row_delta)).astype(jnp.bfloat16)
    query_gradient_rows = (
        jnp.einsum(
            "luar,lurs->las", score_gradient, windowed_keys, preferred_element_type=jnp.float32
        )
        * logit_scale
    )
    windowed_key_gradient = (
        jnp.einsum(
            "gxin,gie->gxne", score_gradient, query_matrix, preferred_element_type=jnp.float32
        )
        * logit_scale
    )
    windowed_value_gradient = jnp.einsum(
        "gxin,gie->gxne", backward_probability, output_gradient, preferred_element_type=jnp.float32
    )
    key_grad = sum(
        (
            jnp.pad(
                windowed_key_gradient[:, offset], ((offset, tile_span - 1 - offset), (0, 0), (0, 0))
            )
            for offset in range(tile_span)
        )
    )
    value_grad = sum(
        (
            jnp.pad(
                windowed_value_gradient[:, offset],
                ((offset, tile_span - 1 - offset), (0, 0), (0, 0)),
            )
            for offset in range(tile_span)
        )
    )
    return (query_gradient_rows, key_grad, value_grad)


def block_mask(tile_mask, head_index, first_block, block_count, all_blocks):
    tile_span = tile_mask.shape[2]
    reach_blocks = tile_span // 2
    mask_head = lax.dynamic_index_in_dim(tile_mask, head_index, 0, keepdims=False)
    padded = jnp.pad(mask_head, ((2 * reach_blocks, 2 * reach_blocks), (0, 0)))
    local_mask = lax.dynamic_slice_in_dim(padded, first_block + 2 * reach_blocks, block_count, 0)
    query_block = first_block + jnp.arange(block_count, dtype=jnp.int32)
    offsets = jnp.arange(tile_span, dtype=jnp.int32) - reach_blocks
    key_block = query_block[:, None] + offsets[None, :]
    key_ok = (key_block >= 0) & (key_block < all_blocks)
    query_ok = (query_block >= 0) & (query_block < all_blocks)
    return jnp.where(query_ok[:, None], (local_mask != 0) & key_ok, offsets[None, :] == 0)


def shards(query, key, value, dout, tile_mask):
    n_uly = lax.axis_size("uly")
    tok_rows, model_width = query.shape
    n_heads = tile_mask.shape[0]
    head_dim = model_width // n_heads
    tile_span = tile_mask.shape[2]
    reach_blocks = tile_span // 2
    block_rows = BLK
    slab_rows = tok_rows * n_uly
    n_blocks = slab_rows // block_rows
    all_blocks = tile_mask.shape[1]
    logit_scale = 1.0 / math.sqrt(head_dim)
    rim_rows = reach_blocks * block_rows
    head_range = jnp.arange(n_heads, dtype=jnp.int32)
    slots_dev = (n_heads + n_uly - 1) // n_uly
    n_slots = n_uly * slots_dev
    slot_ids = jnp.arange(n_slots, dtype=jnp.int32)
    owners = slot_ids // slots_dev
    within = slot_ids % slots_dev
    dealt_head = within * n_uly + owners
    is_live = dealt_head < n_heads
    slot_head = jnp.minimum(dealt_head, n_heads - 1)
    head_hot = (slot_head[:, None] == head_range[None, :]) & is_live[:, None]
    slot_of_head = jnp.sum(jnp.where(head_hot, slot_ids[:, None], 0), 0)
    live_cast = is_live.astype(jnp.bfloat16)[None, :, None]

    def outgoing(source):
        return jnp.take(source.reshape(tok_rows, n_heads, head_dim), slot_head, axis=1) * live_cast

    q_recv, k_recv, v_recv, g_recv = (
        lax.all_to_all(outgoing(query), "uly", split_axis=1, concat_axis=0, tiled=True),
        lax.all_to_all(outgoing(key), "uly", split_axis=1, concat_axis=0, tiled=True),
        lax.all_to_all(outgoing(value), "uly", split_axis=1, concat_axis=0, tiled=True),
        lax.all_to_all(outgoing(dout), "uly", split_axis=1, concat_axis=0, tiled=True),
    )
    my_uly = lax.axis_index("uly")
    my_ctx = lax.axis_index("ctx")
    mine_head = lax.dynamic_slice_in_dim(slot_head, my_uly * slots_dev, slots_dev)
    pair_rows = padded_2(jnp.stack((k_recv, v_recv), 1), (("ctx", 0),), rim_rows)
    query_ext = 0
    n_query = n_blocks + 2 * query_ext
    n_keys = n_query + 2 * reach_blocks
    first_block = my_ctx * n_blocks - query_ext
    query_list = []
    pair_list = []
    for slot_index in range(slots_dev):
        q_rows = q_recv[:, slot_index]
        k_rows = pair_rows[:, 0, slot_index]
        v_rows = pair_rows[:, 1, slot_index]
        g_rows = g_recv[:, slot_index]
        active = block_mask(tile_mask, mine_head[slot_index], first_block, n_query, all_blocks)
        query_gradient_rows, key_grad, value_grad = attend_grad(
            q_rows.reshape(n_query, block_rows, head_dim),
            k_rows.reshape(n_keys, block_rows, head_dim),
            v_rows.reshape(n_keys, block_rows, head_dim),
            g_rows.reshape(n_query, block_rows, head_dim),
            active,
            logit_scale,
        )
        pair_grad = jnp.stack(
            (
                key_grad.reshape(n_keys * block_rows, head_dim),
                value_grad.reshape(n_keys * block_rows, head_dim),
            ),
            1,
        )
        result = (query_gradient_rows.reshape(n_query * block_rows, head_dim), pair_grad)
        query_list.append(result[0])
        pair_list.append(result[1])
    query_grads = jnp.stack(query_list, 1).astype(jnp.bfloat16)
    pair_grads = jnp.stack(pair_list, 2)
    own_rows = pair_grads[rim_rows : rim_rows + slab_rows]
    lower_rim = pair_grads[:rim_rows]
    upper_rim = pair_grads[rim_rows + slab_rows :]
    from_next = passed_along(lower_rim.astype(jnp.bfloat16), "ctx", -1).astype(lower_rim.dtype)
    from_prev = passed_along(upper_rim.astype(jnp.bfloat16), "ctx", 1).astype(upper_rim.dtype)
    own_rows = own_rows.at[:rim_rows].add(from_prev).at[slab_rows - rim_rows :].add(from_next)
    summed = own_rows.astype(jnp.bfloat16)
    back_query, back_key, back_value = (
        lax.all_to_all(query_grads, "uly", split_axis=0, concat_axis=1, tiled=True),
        lax.all_to_all(summed[:, 0], "uly", split_axis=0, concat_axis=1, tiled=True),
        lax.all_to_all(summed[:, 1], "uly", split_axis=0, concat_axis=1, tiled=True),
    )

    def to_tokens(source):
        return jnp.take(source, slot_of_head, axis=1).reshape(tok_rows, model_width)

    return (to_tokens(back_query), to_tokens(back_key), to_tokens(back_value))


def solution(mesh):
    placed = (
        P(("ctx", "uly"), None),
        P(("ctx", "uly"), None),
        P(("ctx", "uly"), None),
        P(("ctx", "uly"), None),
        P(),
    )
    return jax.shard_map(
        shards,
        mesh=mesh,
        in_specs=placed,
        out_specs=(P(("ctx", "uly"), None), P(("ctx", "uly"), None), P(("ctx", "uly"), None)),
        check_vma=False,
    )
```

profile of v0, /device:TPU:0, one launch (start us, length us, event | category | flops | bytes accessed | tf_op | source)
XLA Modules:
  0.0 404.0 jit_solution(5266638643182899811)
XLA Ops:
  1.2 1.8 copy.366
  3.8 2.4 copy.360
  6.2 1.8 copy.361
  8.0 1.8 gather_fusion.2
  9.8 1.9 gather_fusion
  13.3 1.8 gather_fusion.1
  17.7 1.8 gather_fusion.3
  19.5 3.7 bitcast_multiply_fusion.6
  23.2 38.5 %all_to_all.120 = bf16[128,40,128]{2,0,1:T(8,128)(2,1)} all-to-all(bf16[128,40,128]{2,0,1:T(8,128)(2,1)S(1)} %get-tuple-element.166), channel_id=1, replica_groups=mesh['ctx'=4,'uly'=8] {'uly'}, dimensions={1} | all-to-all | bytes 2621440 | tf_op jit(solution)/shard_map/all_to_all | solution.py:135
  61.8 34.5 %all_to_all.121 = bf16[128,40,128]{2,0,1:T(8,128)(2,1)S(1)} all-to-all(bf16[128,40,128]{2,0,1:T(8,128)(2,1)S(1)} %get-tuple-element.167), channel_id=1, replica_groups=mesh['ctx'=4,'uly'=8] {'uly'}, dimensions={1} | all-to-all | bytes 2621440 | tf_op jit(solution)/shard_map/all_to_all | solution.py:137
  96.2 34.4 %all_to_all.122 = bf16[128,40,128]{2,0,1:T(8,128)(2,1)} all-to-all(bf16[128,40,128]{2,0,1:T(8,128)(2,1)S(1)} %get-tuple-element.169), channel_id=1, replica_groups=mesh['ctx'=4,'uly'=8] {'uly'}, dimensions={1} | all-to-all | bytes 2621440 | tf_op jit(solution)/shard_map/all_to_all | solution.py:136
  130.6 4.4 %all-to-all-start.3 = ((bf16[128,40,128]{2,0,1:T(8,128)(2,1)}), bf16[128,40,128]{2,0,1:T(8,128)(2,1)}, u32[]{:S(2)}, u32[]{:S(2)}) async-start(bf16[128,40,128]{2,0,1:T(8,128)(2,1)} %get-tuple-element.168), calls=%async_computation.3 | async-start | bytes 2621440 | tf_op jit(solution)/shard_map/all_to_all | solution.py:138
  150.7 3.9 collective-permute-start
  158.4 7.2 %all-to-all-done.3 = bf16[128,40,128]{2,0,1:T(8,128)(2,1)} async-done(((bf16[128,40,128]{2,0,1:T(8,128)(2,1)}), bf16[128,40,128]{2,0,1:T(8,128)(2,1)}, u32[]{:S(2)}, u32[]{:S(2)}) %all-to-all-start.3) | async-done | bytes 1310752 | tf_op jit(solution)/shard_map/all_to_all | solution.py:138
  167.5 3.4 pad_maximum_fusion
  220.7 10.2 %stack.289 = bf16[1024,5,128]{2,1,0:T(8,128)(2,1)} concatenate(bf16[1024,1,128]{2,1,0:T(2,128)(2,1)} %copy.385, bf16[1024,1,128]{2,1,0:T(2,128)(2,1)} %copy.386, bf16[1024,1,128]{2,1,0:T(2,128)(2,1)} %copy.387, bf16[1024,1,128]{2,1,0:T(2,128)(2,1)} %copy.388, bf16[1024,1,128]{2,1,0:T(2,128)(2,1)S(1)} %copy.389), dimensions={1} | concatenate | bytes 2621440 | tf_op jit(solution)/shard_map/stack | solution.py:174
  230.9 4.3 %all-to-all-start.4 = ((bf16[1024,5,128]{2,1,0:T(8,128)(2,1)}), bf16[1024,5,128]{2,1,0:T(8,128)(2,1)}, u32[]{:S(2)}, u32[]{:S(2)}) async-start(bf16[1024,5,128]{2,1,0:T(8,128)(2,1)} %stack.289), calls=%async_computation.4 | async-start | bytes 4194304 | tf_op jit(solution)/shard_map/all_to_all | solution.py:184
  255.6 3.6 collective-permute-done.3
  260.2 2.3 copy.437
  262.5 20.4 %all-to-all-done.4 = bf16[1024,5,128]{2,1,0:T(8,128)(2,1)} async-done(((bf16[1024,5,128]{2,1,0:T(8,128)(2,1)}), bf16[1024,5,128]{2,1,0:T(8,128)(2,1)}, u32[]{:S(2)}, u32[]{:S(2)}) %all-to-all-start.4) | async-done | bytes 1310752 | tf_op jit(solution)/shard_map/all_to_all | solution.py:184
  282.8 3.6 all-to-all-start.6
  286.5 2.3 copy.433
  288.8 46.1 %all-to-all-done.6 = bf16[1024,5,128]{2,1,0:T(8,128)(2,1)S(1)} async-done(((bf16[1024,5,128]{2,1,0:T(8,128)(2,1)}), bf16[1024,5,128]{2,1,0:T(8,128)(2,1)S(1)}, u32[]{:S(2)}, u32[]{:S(2)}) %all-to-all-start.6) | async-done | bytes 1310752 | tf_op jit(solution)/shard_map/all_to_all | solution.py:186
  334.9 4.3 %all-to-all-start.5 = ((bf16[1024,5,128]{2,1,0:T(8,128)(2,1)}), bf16[1024,5,128]{2,1,0:T(8,128)(2,1)}, u32[]{:S(2)}, u32[]{:S(2)}) async-start(bf16[1024,5,128]{2,1,0:T(8,128)(2,1)} %copy.433), calls=%async_computation.5 | async-start | bytes 4194304 | tf_op jit(solution)/shard_map/all_to_all | solution.py:185
  339.4 1.9 copy.391
  341.3 1.9 gather_fusion.4
  343.6 1.9 gather_fusion.6
  345.4 41.7 %all-to-all-done.5 = bf16[1024,5,128]{2,1,0:T(8,128)(2,1)} async-done(((bf16[1024,5,128]{2,1,0:T(8,128)(2,1)}), bf16[1024,5,128]{2,1,0:T(8,128)(2,1)}, u32[]{:S(2)}, u32[]{:S(2)}) %all-to-all-start.5) | async-done | bytes 1310752 | tf_op jit(solution)/shard_map/all_to_all | solution.py:185
  387.1 1.9 copy.435
  389.0 1.9 gather_fusion.5
  390.9 4.0 select_bitcast_fusion
  394.9 1.8 copy.440
  (294 shorter events, 94.6 us)
Async XLA Ops:
  9.8 1.9 copy-start.49
  17.7 1.9 copy-start.2
  130.6 14.6 %copy-start.48 = (s32[40,32,5]{0,1,2:T(8,128)S(1)}, s32[40,32,5]{0,1,2:T(8,128)}, u32[]{:S(2)}) copy-start(s32[40,32,5]{0,1,2:T(8,128)} %param.15) | copy-start | bytes 76804
  130.6 34.9 %all-to-all-start.3 = ((bf16[128,40,128]{2,0,1:T(8,128)(2,1)}), bf16[128,40,128]{2,0,1:T(8,128)(2,1)}, u32[]{:S(2)}, u32[]{:S(2)}) async-start(bf16[128,40,128]{2,0,1:T(8,128)(2,1)} %get-tuple-element.168), calls=%async_computation.3 | async-start | bytes 2621440 | tf_op jit(solution)/shard_map/all_to_all | solution.py:138
  149.4 18.1 %collective-permute-start.1 = (bf16[256,2,5,128]{3,0,2,1:T(8,128)(2,1)}, bf16[256,2,5,128]{3,0,2,1:T(8,128)(2,1)}, u32[]{:S(2)}, u32[]{:S(2)}) collective-permute-start(bf16[256,2,5,128]{3,0,2,1:T(8,128)(2,1)} %get-tuple-element.134), channel_id=1, source_target_pairs={{8,0},{16,8},{24,16},{9,1},{17,9},{25,17},{10,2},{18,10},{26,18},{... | collective-permute-start | bytes 1966088 | tf_op jit(solution)/shard_map/ppermute | solution.py:19
  150.7 16.8 %collective-permute-start = (bf16[256,2,5,128]{3,0,2,1:T(8,128)(2,1)}, bf16[256,2,5,128]{3,0,2,1:T(8,128)(2,1)}, u32[]{:S(2)}, u32[]{:S(2)}) collective-permute-start(bf16[256,2,5,128]{3,0,2,1:T(8,128)(2,1)} %get-tuple-element.135), channel_id=1, source_target_pairs={{0,8},{8,16},{16,24},{1,9},{9,17},{17,25},{2,10},{10,18},{18,26},{... | collective-permute-start | bytes 1966088 | tf_op jit(solution)/shard_map/ppermute | solution.py:18
  155.5 1.7 copy-start
  165.6 1.7 copy-start.1
  230.9 51.9 %all-to-all-start.4 = ((bf16[1024,5,128]{2,1,0:T(8,128)(2,1)}), bf16[1024,5,128]{2,1,0:T(8,128)(2,1)}, u32[]{:S(2)}, u32[]{:S(2)}) async-start(bf16[1024,5,128]{2,1,0:T(8,128)(2,1)} %stack.289), calls=%async_computation.4 | async-start | bytes 4194304 | tf_op jit(solution)/shard_map/all_to_all | solution.py:184
  235.3 1.5 copy-start.46
  235.3 1.6 copy-start.47
  237.3 1.5 copy-start.36
  237.3 1.6 copy-start.37
  238.9 1.5 copy-start.41
  238.9 1.7 copy-start.42
  240.8 1.5 copy-start.26
  240.8 1.6 copy-start.27
  242.4 1.5 copy-start.31
  242.4 1.7 copy-start.32
  244.3 1.5 copy-start.16
  244.3 1.6 copy-start.17
  245.9 1.5 copy-start.21
  245.9 1.7 copy-start.22
  247.8 1.5 copy-start.6
  247.8 1.6 copy-start.7
  249.4 1.5 copy-start.11
  249.4 1.7 copy-start.12
  252.2 3.3 collective-permute-start.2
  253.5 5.7 %collective-permute-start.3 = (bf16[256,2,5,128]{3,0,2,1:T(8,128)(2,1)S(1)}, bf16[256,2,5,128]{3,0,2,1:T(8,128)(2,1)S(1)}, u32[]{:S(2)}, u32[]{:S(2)}) collective-permute-start(bf16[256,2,5,128]{3,0,2,1:T(8,128)(2,1)S(1)} %get-tuple-element.40), channel_id=1, source_target_pairs={{8,0},{16,8},{24,16},{9,1},{17,9},{25,17},{10,2},{18,10},{26,18},{... | collective-permute-start | bytes 1966088 | tf_op jit(solution)/shard_map/ppermute | solution.py:27
  282.8 52.0 %all-to-all-start.6 = ((bf16[1024,5,128]{2,1,0:T(8,128)(2,1)}), bf16[1024,5,128]{2,1,0:T(8,128)(2,1)S(1)}, u32[]{:S(2)}, u32[]{:S(2)}) async-start(bf16[1024,5,128]{2,1,0:T(8,128)(2,1)} %copy.437), calls=%async_computation.6 | async-start | bytes 4194304 | tf_op jit(solution)/shard_map/all_to_all | solution.py:186
  288.8 50.5 %copy-start.57 = (pred[40]{0:T(512)(128)(4,1)S(1)}, pred[40]{0:T(512)(128)(4,1)}, u32[]{:S(2)}) copy-start(pred[40]{0:T(512)(128)(4,1)} %get-tuple-element.201) | copy-start | bytes 124
  334.9 52.2 %all-to-all-start.5 = ((bf16[1024,5,128]{2,1,0:T(8,128)(2,1)}), bf16[1024,5,128]{2,1,0:T(8,128)(2,1)}, u32[]{:S(2)}, u32[]{:S(2)}) async-start(bf16[1024,5,128]{2,1,0:T(8,128)(2,1)} %copy.433), calls=%async_computation.5 | async-start | bytes 4194304 | tf_op jit(solution)/shard_map/all_to_all | solution.py:185
  (34 other events, 39.1 us)
where the time goes:
time: 412 us; the launch traced here: 404 us
  waiting for transfers between devices  119 us (29%)
  blocking collectives  107 us (26%)
  local copies, waits for them, and re-layouts  99.8 us (24%)
  other arithmetic  25.1 us (6%)
  starting transfers between devices  24.7 us (6%)
  matrix products  15.9 us (4%)
  between operations  12 us (3%)
    all_to_all x1, waiting for transfers between devices, shards(): lax.all_to_all(summed[:, 1], 'uly', split_axis=0, concat_axis=1, tiled=True)  46.1 us
    all_to_all x1, waiting for transfers between devices, shards(): lax.all_to_all(summed[:, 0], 'uly', split_axis=0, concat_axis=1, tiled=True)  41.7 us
    all_to_all x1, blocking collectives, shards(): lax.all_to_all(outgoing(query), 'uly', split_axis=1, concat_axis=0, tiled...  38.5 us
    all_to_all x1, blocking collectives, shards(): lax.all_to_all(outgoing(value), 'uly', split_axis=1, concat_axis=0, tiled...  34.5 us
    all_to_all x1, blocking collectives, shards(): lax.all_to_all(outgoing(key), 'uly', split_axis=1, concat_axis=0, tiled=T...  34.4 us
    unnamed x168, local copies, waits for them, and re-layouts  30.7 us
    all_to_all x1, waiting for transfers between devices, shards(): lax.all_to_all(query_grads, 'uly', split_axis=0, concat_axis=1, tiled=True)  20.4 us
    another operation x6, local copies, waits for them, and re-layouts, shards(): query_grads = jnp.stack(query_list, 1).astype(jnp.bfloat16)  15.4 us
  transfers between devices with their start and end apart: 8, of which 5 were waited for; matrix products, arithmetic and copies ran while one was open for 6% of the time, Pallas kernels for 0%

commit v1 on v0

v1 whole, which is shorter than its diff:
```python
import functools
import math

import jax
import jax.numpy as jnp
from jax import lax
from jax.experimental import pallas as pl
from jax.experimental.pallas import tpu as pltpu
from jax.sharding import PartitionSpec as P

BLK = 128
MESH = pl.DeviceIdType.MESH
AHEAD = 2


def kernel(
    dims,
    bias,
    q_in,
    k_in,
    v_in,
    g_in,
    q_out,
    k_out,
    v_out,
    kv,
    qg,
    acc,
    back,
    rim_put,
    rim_got,
    kv_send,
    kv_recv,
    kv_own,
    qg_send,
    qg_recv,
    qg_own,
    halo_send,
    halo_recv,
    rim_send,
    rim_recv,
    out_send,
    out_recv,
    out_own,
):
    n_ctx, n_uly, tok, hd, slots, span = dims
    rim = span // 2 * BLK
    slab = n_uly * tok
    n_blocks = slab // BLK
    rim_devices = (rim + tok - 1) // tok
    scale = 1.0 / math.sqrt(hd)
    ctx, uly = lax.axis_index("ctx"), lax.axis_index("uly")
    has_prev, has_next = ctx > 0, ctx < n_ctx - 1

    def peer_of(step):
        return lax.rem(uly + step, n_uly)

    def columns(owner, head):
        return pl.ds(pl.multiple_of((owner * slots + head) * hd, hd), hd)

    def own_rows(device):
        return pl.ds(pl.multiple_of(device * tok, tok), tok)

    def ext_rows(device):
        return pl.ds(pl.multiple_of(rim + device * tok, BLK), tok)

    barrier = pltpu.get_barrier_semaphore()

    @pl.loop(1, n_uly)
    def _(step):
        pl.semaphore_signal(
            barrier, inc=1, device_id={"uly": peer_of(step)}, device_id_type=MESH
        )

    @pl.when(has_prev)
    def _():
        pl.semaphore_signal(barrier, inc=1, device_id={"ctx": ctx - 1}, device_id_type=MESH)

    @pl.when(has_next)
    def _():
        pl.semaphore_signal(barrier, inc=1, device_id={"ctx": ctx + 1}, device_id_type=MESH)

    neighbours = has_prev.astype(jnp.int32) + has_next.astype(jnp.int32)
    pl.semaphore_wait(barrier, n_uly - 1 + neighbours)

    def send_head(head):
        for part, source in enumerate((k_in, v_in)):
            pltpu.make_async_copy(
                source.at[:, columns(uly, head)], kv.at[head, part, ext_rows(uly)], kv_own.at[head, part]
            ).start()
        for part, source in enumerate((q_in, g_in)):
            pltpu.make_async_copy(
                source.at[:, columns(uly, head)], qg.at[head, part, own_rows(uly)], qg_own.at[head, part]
            ).start()

        @pl.loop(1, n_uly)
        def _(step):
            peer = peer_of(step)
            for part, source in enumerate((k_in, v_in)):
                pltpu.make_async_remote_copy(
                    src_ref=source.at[:, columns(peer, head)],
                    dst_ref=kv.at[head, part, ext_rows(uly)],
                    send_sem=kv_send.at[head],
                    recv_sem=kv_recv.at[head],
                    device_id={"uly": peer},
                    device_id_type=MESH,
                ).start()
            for part, source in enumerate((q_in, g_in)):
                pltpu.make_async_remote_copy(
                    src_ref=source.at[:, columns(peer, head)],
                    dst_ref=qg.at[head, part, own_rows(uly)],
                    send_sem=qg_send.at[head],
                    recv_sem=qg_recv.at[head],
                    device_id={"uly": peer},
                    device_id_type=MESH,
                ).start()

    def wait_bytes(ref, sem):
        pltpu.make_async_copy(ref, ref, sem).wait()

    def halo_up(head):
        return pltpu.make_async_remote_copy(
            src_ref=kv.at[head, :, pl.ds(slab, rim)],
            dst_ref=kv.at[head, :, pl.ds(0, rim)],
            send_sem=halo_send.at[head, 0],
            recv_sem=halo_recv.at[head, 0],
            device_id={"ctx": ctx + 1},
            device_id_type=MESH,
        )

    def halo_down(head):
        return pltpu.make_async_remote_copy(
            src_ref=kv.at[head, :, pl.ds(rim, rim)],
            dst_ref=kv.at[head, :, pl.ds(rim + slab, rim)],
            send_sem=halo_send.at[head, 1],
            recv_sem=halo_recv.at[head, 1],
            device_id={"ctx": ctx - 1},
            device_id_type=MESH,
        )

    def rim_up(head):
        return pltpu.make_async_remote_copy(
            src_ref=rim_put.at[head, 0],
            dst_ref=rim_got.at[head, 0],
            send_sem=rim_send.at[head, 0],
            recv_sem=rim_recv.at[head, 0],
            device_id={"ctx": ctx + 1},
            device_id_type=MESH,
        )

    def rim_down(head):
        return pltpu.make_async_remote_copy(
            src_ref=rim_put.at[head, 1],
            dst_ref=rim_got.at[head, 1],
            send_sem=rim_send.at[head, 1],
            recv_sem=rim_recv.at[head, 1],
            device_id={"ctx": ctx - 1},
            device_id_type=MESH,
        )

    def send_back(head, peer, parts):
        for part, target in enumerate((q_out, k_out, v_out)):
            if part in parts:
                pltpu.make_async_remote_copy(
                    src_ref=back.at[head, part, own_rows(peer)],
                    dst_ref=target.at[:, columns(uly, head)],
                    send_sem=out_send.at[part],
                    recv_sem=out_recv.at[part],
                    device_id={"uly": peer},
                    device_id_type=MESH,
                ).start()

    def keep(head, parts):
        for part, target in enumerate((q_out, k_out, v_out)):
            if part in parts:
                pltpu.make_async_copy(
                    back.at[head, part, own_rows(uly)],
                    target.at[:, columns(uly, head)],
                    out_own.at[part],
                ).start()

    def is_rim(device):
        return (device < rim_devices) | (device >= n_uly - rim_devices)

    def attend(head):
        acc[...] = jnp.zeros_like(acc)

        @pl.loop(0, n_blocks)
        def _(block):
            row = pl.multiple_of(block * BLK, BLK)
            k_win = kv[head, 0, pl.ds(row, span * BLK), :]
            v_win = kv[head, 1, pl.ds(row, span * BLK), :]
            q = qg[head, 0, pl.ds(row, BLK), :]
            g = qg[head, 1, pl.ds(row, BLK), :]
            nt = (((1,), (1,)), ((), ()))
            logits = lax.dot_general(k_win, q, nt, preferred_element_type=jnp.float32)
            place = (head * n_blocks + block) * span
            logits = jnp.concatenate(
                [logits[o * BLK : (o + 1) * BLK] + bias[place + o] for o in range(span)], axis=0
            )
            top = jnp.max(logits, axis=0, keepdims=True)
            weights = jnp.exp((logits - top) * scale)
            prob = weights * (1.0 / jnp.sum(weights, axis=0, keepdims=True))
            dprob = lax.dot_general(v_win, g, nt, preferred_element_type=jnp.float32)
            delta = jnp.sum(prob * dprob, axis=0, keepdims=True)
            dscore = (prob * (dprob - delta)).astype(jnp.bfloat16)
            prob_b = prob.astype(jnp.bfloat16)
            acc[0, pl.ds(row, span * BLK), :] += jnp.dot(
                dscore, q, preferred_element_type=jnp.float32
            )
            acc[1, pl.ds(row, span * BLK), :] += jnp.dot(
                prob_b, g, preferred_element_type=jnp.float32
            )
            dq = lax.dot_general(
                dscore, k_win, (((0,), (0,)), ((), ())), preferred_element_type=jnp.float32
            )
            back[head, 0, pl.ds(row, BLK), :] = (dq * scale).astype(jnp.bfloat16)

    @pl.when(jnp.logical_not(has_prev))
    def _():
        kv[:, :, :rim, :] = jnp.zeros((slots, 2, rim, hd), jnp.bfloat16)

    @pl.when(jnp.logical_not(has_next))
    def _():
        kv[:, :, rim + slab :, :] = jnp.zeros((slots, 2, rim, hd), jnp.bfloat16)

    @pl.loop(0, min(AHEAD, slots))
    def _(head):
        send_head(head)

    @pl.loop(0, slots)
    def _(head):
        @pl.when(head + AHEAD < slots)
        def _():
            send_head(head + AHEAD)

        for part in range(2):
            wait_bytes(kv.at[head, part, pl.ds(0, tok)], kv_own.at[head, part])
        wait_bytes(kv.at[head, :, pl.ds(0, (n_uly - 1) * tok)], kv_recv.at[head])

        @pl.when(has_next)
        def _():
            halo_up(head).start()

        @pl.when(has_prev)
        def _():
            halo_down(head).start()

        for part in range(2):
            wait_bytes(qg.at[head, part, pl.ds(0, tok)], qg_own.at[head, part])
        wait_bytes(qg.at[head, :, pl.ds(0, (n_uly - 1) * tok)], qg_recv.at[head])

        @pl.when(has_prev)
        def _():
            halo_up(head).wait_recv()

        @pl.when(has_next)
        def _():
            halo_down(head).wait_recv()

        attend(head)
        scales = (scale, 1.0)

        for part in range(2):
            rim_put[head, 0, part] = (acc[part, rim + slab :, :] * scales[part]).astype(jnp.bfloat16)
            rim_put[head, 1, part] = (acc[part, :rim, :] * scales[part]).astype(jnp.bfloat16)

        @pl.when(has_next)
        def _():
            rim_up(head).start()

        @pl.when(has_prev)
        def _():
            rim_down(head).start()

        if slab > 2 * rim:
            for part in range(2):
                back[head, 1 + part, rim : slab - rim, :] = (
                    acc[part, 2 * rim : slab, :] * scales[part]
                ).astype(jnp.bfloat16)

        @pl.loop(1, n_uly)
        def _(step):
            peer = peer_of(step)
            send_back(head, peer, (0,))

            @pl.when(jnp.logical_not(is_rim(peer)))
            def _():
                send_back(head, peer, (1, 2))

        keep(head, (0,))

        for part in range(2):
            first = acc[part, rim : 2 * rim, :] * scales[part]
            last = acc[part, slab : slab + rim, :] * scales[part]
            acc[part, rim : 2 * rim, :] = first
            acc[part, slab : slab + rim, :] = last

        @pl.when(has_prev)
        def _():
            rim_up(head).wait_recv()
            for part in range(2):
                acc[part, rim : 2 * rim, :] += rim_got[head, 0, part].astype(jnp.float32)

        @pl.when(has_next)
        def _():
            rim_down(head).wait_recv()
            for part in range(2):
                acc[part, slab : slab + rim, :] += rim_got[head, 1, part].astype(jnp.float32)

        for part in range(2):
            back[head, 1 + part, :rim, :] = acc[part, rim : 2 * rim, :].astype(jnp.bfloat16)
            back[head, 1 + part, slab - rim :, :] = acc[part, slab : slab + rim, :].astype(
                jnp.bfloat16
            )
        keep(head, (1, 2))

        @pl.loop(1, n_uly)
        def _(step):
            peer = peer_of(step)

            @pl.when(is_rim(peer))
            def _():
                send_back(head, peer, (1, 2))

    @pl.loop(0, slots)
    def _(head):
        wait_bytes(kv.at[head, :, pl.ds(0, (n_uly - 1) * tok)], kv_send.at[head])
        wait_bytes(qg.at[head, :, pl.ds(0, (n_uly - 1) * tok)], qg_send.at[head])

        @pl.when(has_next)
        def _():
            halo_up(head).wait_send()
            rim_up(head).wait_send()

        @pl.when(has_prev)
        def _():
            halo_down(head).wait_send()
            rim_down(head).wait_send()

    for part, target in enumerate((q_out, k_out, v_out)):
        wait_bytes(target.at[:, pl.ds(0, slots * hd)], out_own.at[part])
        wait_bytes(target.at[:, pl.ds(0, (n_uly - 1) * slots * hd)], out_send.at[part])
        wait_bytes(target.at[:, pl.ds(0, (n_uly - 1) * slots * hd)], out_recv.at[part])


def shards(query, key, value, dout, tile_mask):
    n_ctx, n_uly = lax.axis_size("ctx"), lax.axis_size("uly")
    tok, width = query.shape
    n_heads, all_blocks, span = tile_mask.shape
    hd = width // n_heads
    reach = span // 2
    rim = reach * BLK
    slab = tok * n_uly
    n_blocks = slab // BLK
    slots = (n_heads + n_uly - 1) // n_uly
    extra = slots * n_uly - n_heads
    full = slots * n_uly * hd

    mask = jnp.pad(tile_mask, ((0, extra), (0, 0), (0, 0)))
    first_block = lax.axis_index("ctx") * n_blocks
    mask = lax.dynamic_slice(
        mask, (lax.axis_index("uly") * slots, first_block, 0), (slots, n_blocks, span)
    )
    offsets = jnp.arange(span, dtype=jnp.int32) - reach
    key_block = first_block + jnp.arange(n_blocks, dtype=jnp.int32)[:, None] + offsets[None, :]
    key_ok = (key_block >= 0) & (key_block < all_blocks)
    active = ((mask != 0) & key_ok[None]) | (offsets == 0)
    bias = jnp.where(active, 0.0, -jnp.inf).astype(jnp.float32).reshape(-1)

    arrays = (query, key, value, dout)
    if extra:
        arrays = tuple(jnp.pad(a, ((0, 0), (0, extra * hd))) for a in arrays)
    dims = (n_ctx, n_uly, tok, hd, slots, span)
    dma = pltpu.SemaphoreType.DMA
    anywhere = pl.BlockSpec(memory_space=pl.ANY)
    outs = pl.pallas_call(
        functools.partial(kernel, dims),
        out_shape=[jax.ShapeDtypeStruct((tok, full), jnp.bfloat16)] * 3,
        in_specs=[pl.BlockSpec(memory_space=pltpu.SMEM)] + [anywhere] * 4,
        out_specs=[anywhere] * 3,
        scratch_shapes=[
            pltpu.VMEM((slots, 2, slab + 2 * rim, hd), jnp.bfloat16),
            pltpu.VMEM((slots, 2, slab, hd), jnp.bfloat16),
            pltpu.VMEM((2, slab + 2 * rim, hd), jnp.float32),
            pltpu.VMEM((slots, 3, slab, hd), jnp.bfloat16),
            pltpu.VMEM((slots, 2, 2, rim, hd), jnp.bfloat16),
            pltpu.VMEM((slots, 2, 2, rim, hd), jnp.bfloat16),
            dma((slots,)),
            dma((slots,)),
            dma((slots, 2)),
            dma((slots,)),
            dma((slots,)),
            dma((slots, 2)),
            dma((slots, 2)),
            dma((slots, 2)),
            dma((slots, 2)),
            dma((slots, 2)),
            dma((3,)),
            dma((3,)),
            dma((3,)),
        ],
        compiler_params=pltpu.CompilerParams(
            collective_id=0, has_side_effects=True, vmem_limit_bytes=48 * 2**20
        ),
        cost_estimate=pl.CostEstimate(
            flops=10 * slots * slab * span * BLK * hd,
            bytes_accessed=14 * tok * full,
            transcendentals=slots * slab * span * BLK,
        ),
        name="tile_attention_grad",
    )(bias, *arrays)
    return tuple(o[:, :width] for o in outs)


def solution(mesh):
    rows = P(("ctx", "uly"), None)
    return jax.shard_map(
        shards,
        mesh=mesh,
        in_specs=(rows, rows, rows, rows, P()),
        out_specs=(rows, rows, rows),
        check_vma=False,
    )
```

time: 412 us -> 212 us (0.51); the launches traced: 404 us -> 212 us
  Pallas kernels: 0 us -> 206 us
  waiting for transfers between devices: 119 us -> 0 us
  blocking collectives: 107 us -> 0 us
  local copies, waits for them, and re-layouts: 99.8 us -> 4.74 us
  starting transfers between devices: 24.7 us -> 0 us
  other arithmetic: 25.1 us -> 0.9 us
  matrix products: 15.9 us -> 0 us
  between operations: 12 us -> 0.68 us
    pallas_call x0 -> x1, Pallas kernels: none -> 206 us  [shards(): pl.pallas_call(functools.partial(kernel, dims), out_shape=[jax.ShapeDtype...]
    all_to_all x4 -> x0, waiting for transfers between devices: 115 us -> none  [the longest x1 46.1 us: shards(): lax.all_to_all(summed[:, 1], 'uly', split_axis=0, concat_axis=1, tiled=True)]
    all_to_all x3 -> x0, blocking collectives: 107 us -> none  [the longest x1 38.5 us: shards(): lax.all_to_all(outgoing(query), 'uly', split_axis=1, concat_axis=0, tiled...]
    unnamed x168 -> x5, local copies, waits for them, and re-layouts: 30.7 us -> 4.48 us
    squeeze x13 -> x0, local copies, waits for them, and re-layouts: 18.6 us -> none  [the longest x5 7.56 us: attend_grad(): windowed_value_gradient[:, offset]]
    all_to_all x4 -> x0, starting transfers between devices: 16.7 us -> none  [the longest x1 4.39 us: shards(): lax.all_to_all(outgoing(dout), 'uly', split_axis=1, concat_axis=0, tiled=...]
    dot_general x25 -> x0, matrix products: 15.9 us -> none  [the longest x5 4.18 us: attend_grad(): jnp.einsum('mip,mejp->meij', output_gradient, windowed_values, preferred_...]
    another operation x16 -> x0, local copies, waits for them, and re-layouts: 15.8 us -> none  [the longest x6 15.4 us: shards(): query_grads = jnp.stack(query_list, 1).astype(jnp.bfloat16)]
  transfers between devices with their start and end apart: 8 -> 0, of which waited for: 5 -> 0; matrix products, arithmetic and copies ran while one was open for 6% -> 0% of each run, Pallas kernels for 0% -> 0%
where the time goes in v1:
time: 212 us
  Pallas kernels  206 us (97%)
  local copies, waits for them, and re-layouts  4.74 us (2%)
    pallas_call x1, Pallas kernels, shards(): pl.pallas_call(functools.partial(kernel, dims), out_shape=[jax.ShapeDtype...  206 us
    unnamed x5, local copies, waits for them, and re-layouts  4.48 us

profile of v1, /device:TPU:0, one launch (start us, length us, event | category | flops | bytes accessed | tf_op | source)
XLA Modules:
  0.0 212.2 jit_solution(1475089195391937673)
XLA Ops:
  0.7 0.1 fusion.3
  0.7 0.8 fusion.2
  1.6 0.1 copy.8
  1.7 0.1 reshape.53.bias
  1.8 0.0 copy-start
  1.8 1.3 copy-done
  3.1 205.9 %tile_attention_grad.1 = (bf16[128,5120]{1,0:T(8,128)(2,1)S(1)}, bf16[128,5120]{1,0:T(8,128)(2,1)S(1)}, bf16[128,5120]{1,0:T(8,128)(2,1)S(1)}) custom-call(f32[200]{0:T(256)S(1)} %reshape.53.bias, bf16[128,5120]{1,0:T(8,128)(2,1)S(1)} %copy-done, bf16[128,5120]{1,0:T(8,128)(2,1)} %k_in.1, bf16[128,5120]{1,0:T(8,128)(2,1)} %v_in.1, bf16[128,5120]{1,0:T(8,128)(2,1)} %g_in.1), custom_call_target="tpu_custom_call" | custom-call | flops 4194304000 | bytes 9175040 | tf_op jit(solution)/shard_map/tile_attention_grad/pallas_call | solution.py:377
  209.0 1.1 copy.12
  210.1 1.1 copy.13
  211.1 1.1 copy.14
  (3 shorter events, 0.0 us)
Async XLA Ops:
  1.8 1.3 copy-start

commit v2 on v0

v2 whole, which is shorter than its diff:
```python
import functools
import math

import jax
import jax.numpy as jnp
from jax import lax
from jax.experimental import pallas as pl
from jax.experimental.pallas import tpu as pltpu
from jax.sharding import PartitionSpec as P

BLK = 128
MESH = pl.DeviceIdType.MESH
NEVER = -1e30
AHEAD = 3
LAG = 2


def kernel(
    dims,
    bias,
    q_in,
    k_in,
    v_in,
    g_in,
    q_out,
    k_out,
    v_out,
    kv,
    qg,
    part_own,
    part_put,
    part_got,
    stat_own,
    stat_got,
    dq_own,
    dq_put,
    dq_got,
    back,
    in_send,
    in_recv,
    in_own,
    qg_send,
    qg_recv,
    part_send,
    part_recv,
    stat_send,
    stat_recv,
    dq_send,
    dq_recv,
    out_send,
    out_recv,
    out_own,
):
    n_ctx, n_uly, tok, hd, slots, group = dims
    rows = group * tok
    nb = rows // BLK
    n_devices = n_ctx * n_uly
    scale = 1.0 / math.sqrt(hd)
    uly = lax.axis_index("uly")
    place = lax.axis_index("ctx") * n_uly + uly
    member = lax.rem(uly, group)
    chunk_start = uly - member
    has_prev = place >= group
    has_next = place < n_devices - group

    def device(index):
        return {"ctx": lax.div(index, n_uly), "uly": lax.rem(index, n_uly)}

    next_id = device(lax.rem(place + group, n_devices))
    prev_id = device(lax.rem(place + n_devices - group, n_devices))

    def columns(owner, head):
        return pl.ds(pl.multiple_of((owner * slots + head) * hd, hd), hd)

    def token_rows(owner):
        return pl.ds(pl.multiple_of(owner * tok, tok), tok)

    def other(step):
        return lax.rem(member + step, group)

    barrier = pltpu.get_barrier_semaphore()
    for step in range(1, group):
        pl.semaphore_signal(
            barrier, inc=1, device_id={"uly": chunk_start + other(step)}, device_id_type=MESH
        )

    @pl.when(has_prev)
    def _():
        pl.semaphore_signal(barrier, inc=1, device_id=prev_id, device_id_type=MESH)

    @pl.when(has_next)
    def _():
        pl.semaphore_signal(barrier, inc=1, device_id=next_id, device_id_type=MESH)

    neighbours = has_prev.astype(jnp.int32) + has_next.astype(jnp.int32)
    pl.semaphore_wait(barrier, group - 1 + neighbours)

    def wait_bytes(ref, sem):
        pltpu.make_async_copy(ref, ref, sem).wait()

    def landing(head, part, owner):
        return (
            kv.at[head, part, token_rows(owner)]
            if part < 2
            else qg.at[head, 1, part - 2, token_rows(owner)]
        )

    def send_in(head):
        for part, source in enumerate((k_in, v_in, q_in, g_in)):
            pltpu.make_async_copy(
                source.at[:, columns(member, head)],
                landing(head, part, member),
                in_own.at[head, part],
            ).start()
            for step in range(1, group):
                pltpu.make_async_remote_copy(
                    src_ref=source.at[:, columns(other(step), head)],
                    dst_ref=landing(head, part, member),
                    send_sem=in_send.at[part],
                    recv_sem=in_recv.at[head, part],
                    device_id={"uly": chunk_start + other(step)},
                    device_id_type=MESH,
                ).start()

    def to_both(sources, targets, send_sem, recv_sem, head):
        for side, there, exists in ((0, next_id, has_next), (1, prev_id, has_prev)):

            @pl.when(exists)
            def _():
                pltpu.make_async_remote_copy(
                    src_ref=sources[side],
                    dst_ref=targets[side],
                    send_sem=send_sem.at[side],
                    recv_sem=recv_sem.at[head, side],
                    device_id=there,
                    device_id_type=MESH,
                ).start()

    def from_both(targets, recv_sem, head):
        for side, exists in ((0, has_prev), (1, has_next)):

            @pl.when(exists)
            def _():
                wait_bytes(targets[side], recv_sem.at[head, side])

    def sides(ref, head):
        return (ref.at[head, 0], ref.at[head, 1])

    def outer_qg(head):
        return (qg.at[head, 0], qg.at[head, 2])

    def forward(head):
        for part in range(4):
            ref = kv.at[head, part] if part < 2 else qg.at[head, 1, part - 2]
            wait_bytes(ref.at[pl.ds(0, tok)], in_own.at[head, part])
            if group > 1:
                wait_bytes(ref.at[pl.ds(0, (group - 1) * tok)], in_recv.at[head, part])
        to_both((qg.at[head, 1], qg.at[head, 1]), outer_qg(head), qg_send, qg_recv, head)

    def logits_of(head, position):
        nt = (((1,), (1,)), ((), ()))
        k, v = kv[head, 0], kv[head, 1]
        q, g = qg[head, position, 0], qg[head, position, 1]
        raw = lax.dot_general(k, q, nt, preferred_element_type=jnp.float32)
        first = (head * 3 + position) * nb * nb
        raw = jnp.concatenate(
            [
                jnp.concatenate(
                    [
                        raw[i * BLK : (i + 1) * BLK, j * BLK : (j + 1) * BLK]
                        + bias[first + j * nb + i]
                        for j in range(nb)
                    ],
                    axis=1,
                )
                for i in range(nb)
            ],
            axis=0,
        )
        dprob = lax.dot_general(v, g, nt, preferred_element_type=jnp.float32)
        return k, q, g, raw, dprob

    def packed(values):
        pieces = [v[:, j * BLK : (j + 1) * BLK] for v in values for j in range(nb)]
        pad = part_own.shape[1] - len(pieces)
        if pad:
            pieces.append(jnp.zeros((pad, BLK), jnp.float32))
        return jnp.concatenate(pieces, axis=0)

    def unpacked(tile, which):
        return jnp.concatenate(
            [tile[which * nb + j : which * nb + j + 1] for j in range(nb)], axis=1
        )

    def partial_stats(head):
        from_both(outer_qg(head), qg_recv, head)
        for position in range(3):
            _, _, _, raw, dprob = logits_of(head, position)
            top = jnp.max(raw, axis=0, keepdims=True)
            weights = jnp.exp((raw - top) * scale)
            total = jnp.sum(weights, axis=0, keepdims=True)
            mixed = jnp.sum(weights * dprob, axis=0, keepdims=True)
            tile = packed((top, total, mixed))
            if position == 1:
                part_own[head] = tile
            else:
                part_put[head, 0 if position == 2 else 1] = tile
        to_both(sides(part_put, head), sides(part_got, head), part_send, part_recv, head)

    def final_stats(head):
        from_both(sides(part_got, head), part_recv, head)
        tiles = (part_own[head], part_got[head, 0], part_got[head, 1])
        tops = [t[:nb] for t in tiles]
        top = jnp.maximum(jnp.maximum(tops[0], tops[1]), tops[2])
        factors = [jnp.exp((t - top) * scale) for t in tops]
        total = sum(t[nb : 2 * nb] * f for t, f in zip(tiles, factors))
        mixed = sum(t[2 * nb : 3 * nb] * f for t, f in zip(tiles, factors))
        inverse = 1.0 / total
        pieces = [top, inverse, mixed * inverse]
        pad = part_own.shape[1] - 3 * nb
        if pad:
            pieces.append(jnp.zeros((pad, BLK), jnp.float32))
        stat_own[head] = jnp.concatenate(pieces, axis=0)
        own = (stat_own.at[head], stat_own.at[head])
        to_both(own, sides(stat_got, head), stat_send, stat_recv, head)

    def gather_out(head, parts):
        for part, target in enumerate((q_out, k_out, v_out)):
            if part not in parts:
                continue
            pltpu.make_async_copy(
                back.at[head, part, token_rows(member)],
                target.at[:, columns(member, head)],
                out_own.at[part],
            ).start()
            for step in range(1, group):
                pltpu.make_async_remote_copy(
                    src_ref=back.at[head, part, token_rows(other(step))],
                    dst_ref=target.at[:, columns(member, head)],
                    send_sem=out_send.at[part],
                    recv_sem=out_recv.at[part],
                    device_id={"uly": chunk_start + other(step)},
                    device_id_type=MESH,
                ).start()

    def gradients(head):
        from_both(sides(stat_got, head), stat_recv, head)
        dk = jnp.zeros((rows, hd), jnp.float32)
        dv = jnp.zeros((rows, hd), jnp.float32)
        for position in range(3):
            tile = stat_own[head] if position == 1 else stat_got[head, position // 2]
            k, q, g, raw, dprob = logits_of(head, position)
            prob = jnp.exp((raw - unpacked(tile, 0)) * scale) * unpacked(tile, 1)
            dscore = (prob * (dprob - unpacked(tile, 2))).astype(jnp.bfloat16)
            dk += jnp.dot(dscore, q, preferred_element_type=jnp.float32)
            dv += jnp.dot(prob.astype(jnp.bfloat16), g, preferred_element_type=jnp.float32)
            tn = (((0,), (0,)), ((), ()))
            dq = lax.dot_general(dscore, k, tn, preferred_element_type=jnp.float32) * scale
            if position == 1:
                dq_own[head] = dq
            else:
                dq_put[head, 0 if position == 2 else 1] = dq.astype(jnp.bfloat16)
        to_both(sides(dq_put, head), sides(dq_got, head), dq_send, dq_recv, head)
        back[head, 1] = (dk * scale).astype(jnp.bfloat16)
        back[head, 2] = dv.astype(jnp.bfloat16)
        gather_out(head, (1, 2))

    def finish(head):
        from_both(sides(dq_got, head), dq_recv, head)
        dq = dq_own[head] + dq_got[head, 0].astype(jnp.float32)
        back[head, 0] = (dq + dq_got[head, 1].astype(jnp.float32)).astype(jnp.bfloat16)
        gather_out(head, (0,))

    for side, exists in ((0, has_prev), (1, has_next)):

        @pl.when(jnp.logical_not(exists))
        def _():
            @pl.loop(0, slots)
            def _(head):
                qg[head, 2 * side] = jnp.zeros((2, rows, hd), jnp.bfloat16)
                part_got[head, side] = jnp.full(part_own.shape[1:], NEVER, jnp.float32)
                stat_got[head, side] = jnp.zeros(part_own.shape[1:], jnp.float32)
                dq_got[head, side] = jnp.zeros((rows, hd), jnp.bfloat16)

    @pl.loop(0, min(AHEAD, slots))
    def _(head):
        send_in(head)

    stages = ((0, forward), (LAG, partial_stats), (LAG + 1, final_stats), (LAG + 2, gradients), (LAG + 3, finish))

    @pl.loop(0, slots + LAG + 3)
    def _(turn):
        @pl.when(turn + AHEAD < slots)
        def _():
            send_in(turn + AHEAD)

        for lag, stage in stages:

            @pl.when((turn >= lag) & (turn < slots + lag))
            def _():
                stage(turn - lag)

    far = (group - 1) * slots * hd
    for part, target in enumerate((q_out, k_out, v_out)):
        wait_bytes(target.at[:, pl.ds(0, slots * hd)], out_own.at[part])
        if group > 1:
            wait_bytes(target.at[:, pl.ds(0, far)], out_send.at[part])
            wait_bytes(target.at[:, pl.ds(0, far)], out_recv.at[part])
    if group > 1:
        for part in range(4):
            wait_bytes(k_in.at[:, pl.ds(0, far)], in_send.at[part])
    for side, exists in ((0, has_next), (1, has_prev)):

        @pl.when(exists)
        def _():
            wait_bytes(qg.at[:, 1], qg_send.at[side])
            wait_bytes(part_put.at[:, side], part_send.at[side])
            wait_bytes(stat_own, stat_send.at[side])
            wait_bytes(dq_put.at[:, side], dq_send.at[side])


def shards(query, key, value, dout, tile_mask):
    n_ctx, n_uly = lax.axis_size("ctx"), lax.axis_size("uly")
    tok, width = query.shape
    n_heads, _, span = tile_mask.shape
    hd = width // n_heads
    reach = span // 2
    group = reach * BLK // tok
    rows = group * tok
    nb = rows // BLK
    slots = (n_heads + group - 1) // group
    extra = slots * group - n_heads
    full = slots * group * hd

    place = lax.axis_index("ctx") * n_uly + lax.axis_index("uly")
    chunk, member = place // group, place % group
    mask = jnp.pad(tile_mask, ((0, extra), (nb, nb), (0, 0)))
    mask = lax.dynamic_slice(mask, (member * slots, chunk * nb, 0), (slots, 3 * nb, span))
    none = jnp.zeros((slots,), tile_mask.dtype)
    pairs = [
        mask[:, j, nb + i - j + reach] if 0 <= nb + i - j + reach < span else none
        for j in range(3 * nb)
        for i in range(nb)
    ]
    bias = jnp.where(jnp.stack(pairs, 1) != 0, 0.0, NEVER).astype(jnp.float32).reshape(-1)

    arrays = (query, key, value, dout)
    if extra:
        arrays = tuple(jnp.pad(a, ((0, 0), (0, extra * hd))) for a in arrays)
    dims = (n_ctx, n_uly, tok, hd, slots, group)
    stat_rows = (3 * nb + 7) // 8 * 8
    dma = pltpu.SemaphoreType.DMA
    anywhere = pl.BlockSpec(memory_space=pl.ANY)
    outs = pl.pallas_call(
        functools.partial(kernel, dims),
        out_shape=[jax.ShapeDtypeStruct((tok, full), jnp.bfloat16)] * 3,
        in_specs=[pl.BlockSpec(memory_space=pltpu.SMEM)] + [anywhere] * 4,
        out_specs=[anywhere] * 3,
        scratch_shapes=[
            pltpu.VMEM((slots, 2, rows, hd), jnp.bfloat16),
            pltpu.VMEM((slots, 3, 2, rows, hd), jnp.bfloat16),
            pltpu.VMEM((slots, stat_rows, BLK), jnp.float32),
            pltpu.VMEM((slots, 2, stat_rows, BLK), jnp.float32),
            pltpu.VMEM((slots, 2, stat_rows, BLK), jnp.float32),
            pltpu.VMEM((slots, stat_rows, BLK), jnp.float32),
            pltpu.VMEM((slots, 2, stat_rows, BLK), jnp.float32),
            pltpu.VMEM((slots, rows, hd), jnp.float32),
            pltpu.VMEM((slots, 2, rows, hd), jnp.bfloat16),
            pltpu.VMEM((slots, 2, rows, hd), jnp.bfloat16),
            pltpu.VMEM((slots, 3, rows, hd), jnp.bfloat16),
            dma((4,)),
            dma((slots, 4)),
            dma((slots, 4)),
            dma((2,)),
            dma((slots, 2)),
            dma((2,)),
            dma((slots, 2)),
            dma((2,)),
            dma((slots, 2)),
            dma((2,)),
            dma((slots, 2)),
            dma((3,)),
            dma((3,)),
            dma((3,)),
        ],
        compiler_params=pltpu.CompilerParams(
            collective_id=0, has_side_effects=True, vmem_limit_bytes=48 * 2**20
        ),
        cost_estimate=pl.CostEstimate(
            flops=42 * slots * rows * rows * hd,
            bytes_accessed=14 * tok * full,
            transcendentals=6 * slots * rows * rows,
        ),
        name="tile_attention_grad",
    )(bias, *arrays)
    return tuple(o[:, :width] for o in outs)


def solution(mesh):
    rows = P(("ctx", "uly"), None)
    return jax.shard_map(
        shards,
        mesh=mesh,
        in_specs=(rows, rows, rows, rows, P()),
        out_specs=(rows, rows, rows),
        check_vma=False,
    )
```

time: 412 us -> 203 us (0.49); the launches traced: 404 us -> 200 us
  Pallas kernels: 0 us -> 192 us
  waiting for transfers between devices: 119 us -> 0 us
  blocking collectives: 107 us -> 0 us
  local copies, waits for them, and re-layouts: 99.8 us -> 6.41 us
  other arithmetic: 25.1 us -> 0.01 us
  starting transfers between devices: 24.7 us -> 0 us
  matrix products: 15.9 us -> 0 us
  between operations: 12 us -> 0.68 us
    pallas_call x0 -> x1, Pallas kernels: none -> 192 us  [shards(): pl.pallas_call(functools.partial(kernel, dims), out_shape=[jax.ShapeDtype...]
    all_to_all x4 -> x0, waiting for transfers between devices: 115 us -> none  [the longest x1 46.1 us: shards(): lax.all_to_all(summed[:, 1], 'uly', split_axis=0, concat_axis=1, tiled=True)]
    all_to_all x3 -> x0, blocking collectives: 107 us -> none  [the longest x1 38.5 us: shards(): lax.all_to_all(outgoing(query), 'uly', split_axis=1, concat_axis=0, tiled...]
    unnamed x168 -> x5, local copies, waits for them, and re-layouts: 30.7 us -> 4.48 us
    squeeze x13 -> x0, local copies, waits for them, and re-layouts: 18.6 us -> none  [the longest x5 7.56 us: attend_grad(): windowed_value_gradient[:, offset]]
    all_to_all x4 -> x0, starting transfers between devices: 16.7 us -> none  [the longest x1 4.39 us: shards(): lax.all_to_all(outgoing(dout), 'uly', split_axis=1, concat_axis=0, tiled=...]
    dot_general x25 -> x0, matrix products: 15.9 us -> none  [the longest x5 4.18 us: attend_grad(): jnp.einsum('mip,mejp->meij', output_gradient, windowed_values, preferred_...]
    another operation x16 -> x4, local copies, waits for them, and re-layouts: 15.8 us -> 1.74 us  [the longest x3 1.74 us: shards(): jnp.stack(pairs, 1) != 0]
  transfers between devices with their start and end apart: 8 -> 0, of which waited for: 5 -> 0; matrix products, arithmetic and copies ran while one was open for 6% -> 0% of each run, Pallas kernels for 0% -> 0%
where the time goes in v2:
time: 203 us; the launch traced here: 200 us
  Pallas kernels  192 us (95%)
  local copies, waits for them, and re-layouts  6.41 us (3%)
    pallas_call x1, Pallas kernels, shards(): pl.pallas_call(functools.partial(kernel, dims), out_shape=[jax.ShapeDtype...  192 us
    unnamed x5, local copies, waits for them, and re-layouts  4.48 us

profile of v2, /device:TPU:0, one launch (start us, length us, event | category | flops | bytes accessed | tf_op | source)
XLA Modules:
  0.0 199.5 jit_solution(16794708694407876333)
XLA Ops:
  0.7 0.8 fusion.2
  1.4 0.9 fusion
  2.4 0.1 copy.8
  2.5 0.1 select_n.30.bias
  2.6 0.0 copy-start
  2.6 1.3 copy-done
  3.9 192.4 %tile_attention_grad.1 = (bf16[128,5120]{1,0:T(8,128)(2,1)S(1)}, bf16[128,5120]{1,0:T(8,128)(2,1)S(1)}, bf16[128,5120]{1,0:T(8,128)(2,1)S(1)}) custom-call(f32[240]{0:T(256)S(1)} %select_n.30.bias, bf16[128,5120]{1,0:T(8,128)(2,1)S(1)} %copy-done, bf16[128,5120]{1,0:T(8,128)(2,1)} %k_in.1, bf16[128,5120]{1,0:T(8,128)(2,1)} %v_in.1, bf16[128,5120]{1,0:T(8,128)(2,1)} %g_in.1), custom_call_target="tpu_custom_call" | custom-call | flops 7046430720 | bytes 9175040 | tf_op jit(solution)/shard_map/tile_attention_grad/pallas_call | solution.py:354
  196.4 1.1 copy.12
  197.4 1.1 copy.13
  198.5 1.1 copy.14
  (3 shorter events, 0.1 us)
Async XLA Ops:
  2.6 1.3 copy-start

commit v3 on v2

--- a/solution.py
+++ b/solution.py
@@ -143,6 +143,9 @@
             def _():
                 wait_bytes(targets[side], recv_sem.at[head, side])
 
+    def stat_sides(ref, head):
+        return (ref.at[head, 0, pl.ds(0, 3 * nb)], ref.at[head, 1, pl.ds(0, 3 * nb)])
+
     def sides(ref, head):
         return (ref.at[head, 0], ref.at[head, 1])
 
@@ -205,10 +208,10 @@
                 part_own[head] = tile
             else:
                 part_put[head, 0 if position == 2 else 1] = tile
-        to_both(sides(part_put, head), sides(part_got, head), part_send, part_recv, head)
+        to_both(stat_sides(part_put, head), stat_sides(part_got, head), part_send, part_recv, head)
 
     def final_stats(head):
-        from_both(sides(part_got, head), part_recv, head)
+        from_both(stat_sides(part_got, head), part_recv, head)
         tiles = (part_own[head], part_got[head, 0], part_got[head, 1])
         tops = [t[:nb] for t in tiles]
         top = jnp.maximum(jnp.maximum(tops[0], tops[1]), tops[2])
@@ -221,8 +224,8 @@
         if pad:
             pieces.append(jnp.zeros((pad, BLK), jnp.float32))
         stat_own[head] = jnp.concatenate(pieces, axis=0)
-        own = (stat_own.at[head], stat_own.at[head])
-        to_both(own, sides(stat_got, head), stat_send, stat_recv, head)
+        own = (stat_own.at[head, pl.ds(0, 3 * nb)],) * 2
+        to_both(own, stat_sides(stat_got, head), stat_send, stat_recv, head)
 
     def gather_out(head, parts):
         for part, target in enumerate((q_out, k_out, v_out)):
@@ -244,7 +247,7 @@
                 ).start()
 
     def gradients(head):
-        from_both(sides(stat_got, head), stat_recv, head)
+        from_both(stat_sides(stat_got, head), stat_recv, head)
         dk = jnp.zeros((rows, hd), jnp.float32)
         dv = jnp.zeros((rows, hd), jnp.float32)
         for position in range(3):
@@ -314,8 +317,8 @@
         @pl.when(exists)
         def _():
             wait_bytes(qg.at[:, 1], qg_send.at[side])
-            wait_bytes(part_put.at[:, side], part_send.at[side])
-            wait_bytes(stat_own, stat_send.at[side])
+            wait_bytes(part_put.at[:, side, pl.ds(0, 3 * nb)], part_send.at[side])
+            wait_bytes(stat_own.at[:, pl.ds(0, 3 * nb)], stat_send.at[side])
             wait_bytes(dq_put.at[:, side], dq_send.at[side])
 
 

time: 203 us -> 202 us (level)
  the two profiles are of different devices: /device:TPU:0 before, /device:TPU:4 now
where the time goes in v3:
time: 202 us
  Pallas kernels  194 us (96%)
  local copies, waits for them, and re-layouts  6.43 us (3%)
    pallas_call x1, Pallas kernels, shards(): pl.pallas_call(functools.partial(kernel, dims), out_shape=[jax.ShapeDtype...  194 us
    unnamed x5, local copies, waits for them, and re-layouts  4.48 us

profile of v3, /device:TPU:4, one launch (start us, length us, event | category | flops | bytes accessed | tf_op | source)
XLA Modules:
  0.0 201.5 jit_solution(11727644795337500358)
XLA Ops:
  0.7 0.8 fusion.2
  1.4 0.9 fusion
  2.4 0.1 copy.8
  2.5 0.1 select_n.30.bias
  2.6 0.0 copy-start
  2.6 1.3 copy-done
  3.9 194.4 %tile_attention_grad.1 = (bf16[128,5120]{1,0:T(8,128)(2,1)S(1)}, bf16[128,5120]{1,0:T(8,128)(2,1)S(1)}, bf16[128,5120]{1,0:T(8,128)(2,1)S(1)}) custom-call(f32[240]{0:T(256)S(1)} %select_n.30.bias, bf16[128,5120]{1,0:T(8,128)(2,1)S(1)} %copy-done, bf16[128,5120]{1,0:T(8,128)(2,1)} %k_in.1, bf16[128,5120]{1,0:T(8,128)(2,1)} %v_in.1, bf16[128,5120]{1,0:T(8,128)(2,1)} %g_in.1), custom_call_target="tpu_custom_call" | custom-call | flops 7046430720 | bytes 9175040 | tf_op jit(solution)/shard_map/tile_attention_grad/pallas_call | solution.py:357
  198.4 1.1 copy.12
  199.4 1.1 copy.13
  200.5 1.1 copy.14
  (3 shorter events, 0.1 us)
Async XLA Ops:
  2.6 1.3 copy-start
